TPU v7x, 512 devices: a whole 4x8x8 slice. The times are simulated.
512 devices in a mesh: fsdp: 32 (over x, y), tensor: 16 (over z, core).
Axes of the slice: x: 4, y: 8, z: 8, core: 2. Of those that a mesh axis runs over, the one named last changes fastest.
Arguments:
- momentum: bfloat16 [8192, 26624], P('fsdp', 'tensor'), may hold values from -360 to 360
- weights: float32 [8192, 26624], P('fsdp', 'tensor'), may hold values from -3 to 3
- basis: float32 [26624, 128], P('tensor', 'fsdp'), may hold values from -6 to 6
Outputs:
- new_weights: float32 [8192, 26624], P('fsdp', 'tensor')
- new_momentum: bfloat16 [8192, 26624], P('fsdp', 'tensor')
- new_basis: float32 [26624, 128], P('tensor', 'fsdp')
All inputs are finite; a program needn't handle non-finite values.
Results may differ from a plain program's by a relative error of at most 0.013.
Values may be sent and summed in bfloat16 or wider, within the bound.
A program may use at most 64 MiB of HBM per device.

v0:
```python
import math

import jax
import jax.numpy as jnp
from jax import lax
from jax.sharding import PartitionSpec as P

DW = 8192
FW = 26624
RANK = 128


HIGH = lax.Precision.HIGHEST


def orthonormalize(block, gram_matrix):
    factor = jnp.linalg.cholesky(gram_matrix)
    return lax.linalg.triangular_solve(factor, block, left_side=False, lower=True, transpose_a=True)


def shards(momentum, weights, basis):
    basis_half = basis.astype(jnp.bfloat16)
    partial_value = jnp.dot(
        momentum,
        lax.all_gather(basis_half, "fsdp", axis=1, tiled=True),
        preferred_element_type=jnp.float32,
    )
    projected = lax.psum(partial_value, "tensor")
    gram_matrix = lax.psum(jnp.dot(projected.T, projected, precision=HIGH), "fsdp")
    ortho = orthonormalize(projected, gram_matrix)
    ortho_half = ortho.astype(jnp.bfloat16)
    local_back = lax.dot_general(
        momentum, ortho_half, (((0,), (0,)), ((), ())), preferred_element_type=jnp.float32
    )
    width = basis.shape[1]
    transposed = lax.psum(local_back.astype(jnp.bfloat16), "fsdp").astype(jnp.float32)
    squares = lax.psum(jnp.sum(transposed * transposed, axis=0), "tensor")
    full_basis = transposed * lax.rsqrt(squares / FW + 1e-06)
    own_basis = lax.dynamic_slice_in_dim(full_basis, lax.axis_index("fsdp") * width, width, 1)
    feedback = lax.dot_general(ortho, transposed, (((1,), (1,)), ((), ())), precision=HIGH)
    new_momentum = (momentum.astype(jnp.float32) - 0.05 * feedback).astype(jnp.bfloat16)
    update = lax.dot_general(ortho, full_basis, (((1,), (1,)), ((), ())), precision=HIGH)
    new_weights = weights - 0.02 * math.sqrt(DW / RANK) * update
    return (new_weights, new_momentum, own_basis)


def solution(mesh):
    in_specs = (P("fsdp", "tensor"), P("fsdp", "tensor"), P("tensor", "fsdp"))
    out_specs = (P("fsdp", "tensor"), P("fsdp", "tensor"), P("tensor", "fsdp"))
    return jax.shard_map(shards, mesh=mesh, in_specs=in_specs, out_specs=out_specs, check_vma=False)
```

profile of v0, /device:TPU:1, one launch (start us, length us, event | category | flops | bytes accessed | tf_op | source)
XLA Modules:
  0.0 553.9 jit_solution(7373952609925228160)
XLA Ops:
  7.2 0.7 convert_bitcast_fusion
  8.0 39.4 %all-gather = bf16[32,4,1664]{2,1,0:T(4,128)(2,1)S(1)} all-gather(bf16[1,4,1664]{2,1,0:T(4,128)(2,1)S(1)} %convert_bitcast_fusion), channel_id=1, replica_groups=mesh['fsdp'=32,'tensor'=16] {'fsdp'}, dimensions={0}, use_global_device_ids=true | all-gather | bytes 439296 | tf_op jit(solution)/shard_map/all_gather | solution.py:25
  47.3 0.1 reshape.17
  47.4 2.3 fusion.10
  49.7 0.0 all-reduce.6.cloned.1.call-start
  49.8 127.2 %all-reduce.4.cloned.1.call-done = f32[256,128]{1,0:T(8,128)} async-done(((f32[256,128]{1,0:T(8,128)}), f32[256,128]{1,0:T(8,128)}) %all-reduce.4.cloned.1.call-update) | async-done | bytes 131088 | tf_op jit(solution)/shard_map/psum | solution.py:28
  177.0 2.0 fusion.11
  179.0 0.0 all-reduce.8.cloned.1.call-start
  179.0 148.5 %all-reduce.6.cloned.1.call-done = f32[128,128]{0,1:T(8,128)} async-done(((f32[128,128]{0,1:T(8,128)}), f32[128,128]{0,1:T(8,128)}) %all-reduce.6.cloned.1.call-update) | async-done | bytes 65552 | tf_op jit(solution)/shard_map/psum | solution.py:29
  327.5 0.9 copy.9
  328.4 0.9 fusion.8
  329.3 11.7 %cholesky.16 = f32[128,128]{1,0:T(8,128)S(1)} custom-call(f32[128,128]{1,0:T(8,128)S(1)} %fusion.8), custom_call_target="Cholesky" | custom-call | tf_op jit(solution)/shard_map/jit(cholesky)/cholesky | solution.py:17
  341.0 0.6 compare_reduce_fusion
  341.7 0.7 fusion.5
  342.4 9.8 %custom-call.6 = f32[1,128,128]{1,2,0:T(8,128)S(1)} custom-call(f32[1,128,128]{2,1,0:T(8,128)S(1)} %fusion.5), custom_call_target="InvertDiagBlocksLowerTriangular" | custom-call | tf_op jit(solution)/shard_map/triangular_solve | solution.py:18
  352.2 1.2 fusion.6
  353.3 1.1 fusion.3
  354.5 156.2 %all-reduce.8.cloned.1.call-done = bf16[1664,128]{0,1:T(8,128)(2,1)} async-done(((bf16[1664,128]{0,1:T(8,128)(2,1)}), bf16[1664,128]{0,1:T(8,128)(2,1)}) %all-reduce.8.cloned.1.call-update) | async-done | bytes 426000 | tf_op jit(solution)/shard_map/psum | solution.py:36
  510.7 1.2 fusion.4
  512.0 28.9 %psum.31 = f32[128]{0:T(128)S(1)} all-reduce(f32[128]{0:T(128)S(1)} %fusion.4), channel_id=1, replica_groups=mesh['fsdp'=32,'tensor'=16] {'tensor'}, use_global_device_ids=true, to_apply=%region_6.7 | all-reduce | flops 128 | bytes 1024 | tf_op jit(solution)/shard_map/psum | solution.py:37
  540.9 1.3 convert_multiply_fusion
  542.1 0.6 constant_dynamic-slice_fusion
  542.8 1.8 fusion.2
  544.5 2.8 fusion.1
  (12 shorter events, 0.1 us)
Async XLA Ops:
  7.2 169.8 %all-reduce.4.cloned.1.call-start = ((), (), s32[]{:S(2)}) async-start(), calls=%async_computation | async-start | bytes 262144 | tf_op jit(solution)/shard_map/psum | solution.py:28
  47.3 306.0 %copy-start = (bf16[256,1664]{1,0:T(8,128)(2,1)S(1)}, bf16[256,1664]{1,0:T(8,128)(2,1)}, u32[]{:S(2)}) copy-start(bf16[256,1664]{1,0:T(8,128)(2,1)} %param.3) | copy-start | bytes 2555908
  49.7 277.8 %all-reduce.6.cloned.1.call-start = ((), (), s32[]{:S(2)}) async-start(), calls=%async_computation.1 | async-start | bytes 131072 | tf_op jit(solution)/shard_map/psum | solution.py:29
  179.0 331.7 %all-reduce.8.cloned.1.call-start = ((), (), s32[]{:S(2)}) async-start(), calls=%async_computation.2 | async-start | bytes 851968 | tf_op jit(solution)/shard_map/psum | solution.py:36
  510.7 32.0 %copy-start.1 = (bf16[1664,128]{0,1:T(8,128)(2,1)S(1)}, bf16[1664,128]{0,1:T(8,128)(2,1)}, u32[]{:S(2)}) copy-start(bf16[1664,128]{0,1:T(8,128)(2,1)} %all-reduce.8.cloned.1.call-done) | copy-start | bytes 1277956
  540.9 3.7 copy-start.2
Sparse Core Ops, SparseCore 0:
  49.8 127.0 all-reduce.3
  181.4 146.0 all-reduce.5
  354.6 156.0 all-reduce.7
where the time goes:
time: 554 us
  waiting for transfers between devices  432 us (78%)
  blocking collectives  68.3 us (12%)
  other arithmetic  27 us (5%)
  between operations  13.8 us (2%)
  matrix products  11.1 us (2%)
    psum x1, waiting for transfers between devices, shards(): lax.psum(local_back.astype(jnp.bfloat16), 'fsdp').astype(jnp.float32)  156 us
    psum x1, waiting for transfers between devices, shards(): lax.psum(jnp.dot(projected.T, projected, precision=HIGH), 'fsdp')  148 us
    psum x1, waiting for transfers between devices, shards(): projected = lax.psum(partial_value, 'tensor')  127 us
    all_gather x1, blocking collectives, shards(): lax.all_gather(basis_half, 'fsdp', axis=1, tiled=True)  39.4 us
    psum x1, blocking collectives, shards(): squares = lax.psum(jnp.sum(transposed * transposed, axis=0), 'tensor')  28.9 us
    another operation x3, other arithmetic, orthonormalize(): factor = jnp.linalg.cholesky(gram_matrix)  12.4 us
  transfers between devices with their start and end apart: 3, of which 3 were waited for; matrix products, arithmetic and copies ran while one was open for 0% of the time, Pallas kernels for 0%

commit v1 on v0

v1 whole, which is shorter than its diff:
```python
import functools
import math

import jax
import jax.numpy as jnp
from jax import lax
from jax.experimental import pallas as pl
from jax.experimental.pallas import tpu as pltpu
from jax.sharding import PartitionSpec as P

DW = 8192
FW = 26624
RANK = 128
ROWS = 256
COLS = 1664
NX, NY, NZ = 4, 8, 8
QUARTER = COLS // NX
SLOT = 64

HIGH = lax.Precision.HIGHEST
MESH = pl.DeviceIdType.MESH
F32 = jnp.float32
BF16 = jnp.bfloat16


def spread_row(a, k):
    return jnp.broadcast_to(a[k : k + 1, :], a.shape)


def inverse_factor(gram):
    lane = lax.broadcasted_iota(jnp.int32, (8, RANK), 1)
    sub = lax.broadcasted_iota(jnp.int32, (8, RANK), 0)
    lanes = lax.broadcasted_iota(jnp.int32, (RANK, RANK), 1)
    rest = gram
    done = []
    for first in range(0, RANK, 8):
        last = first + 8
        panel = rest[first:last, :] if first == 0 else rest[:8, :]
        block = [jnp.broadcast_to(panel[:, first + k : first + k + 1], (8, RANK)) for k in range(8)]
        rows = jnp.where((lane >= first) & (lane < last), jnp.where(lane - first == sub, 1.0, 0.0), panel)
        for k in range(8):
            root = lax.rsqrt(spread_row(block[k], k))
            mult = jnp.where(sub > k, block[k] * (root * root), jnp.where(sub == k, -root, 0.0))
            rows = jnp.where(sub == k, 0.0, rows) - mult * spread_row(rows, k)
            for n in range(k + 1, 8):
                block[n] = block[n] - mult * spread_row(block[n], k)
        done.append(jnp.where(lane < last, rows, 0.0))
        if last < RANK:
            upper = jnp.where(lane >= last, rows, 0.0)
            base = rest[last:, :] if first == 0 else rest[8:, :]
            base = jnp.where((lanes[last:] >= first) & (lanes[last:] < last), 0.0, base)
            change = lax.dot_general(upper, rows, (((0,), (0,)), ((), ())), precision=HIGH, preferred_element_type=F32)
            rest = base - change[last:, :]
    return jnp.concatenate(done, axis=0)


def exchange_kernel(
    momentum_hbm, basis, ortho_out, back_out, scale_out,
    momentum, stage, slots, partial_buf, pair_in, sum_in, projected, gram_buf, gram_x, gram_mid, gram_y, gram_full,
    zq, zx, zmid, zy, back, sq_mine, sq_in,
    load_sem, slot_y_recv, slot_x_recv, slot_send, pair_recv, pair_send, sum_recv, sum_send,
    own_recv, own_send, half_recv, half_send, gx_recv, gx_send, gy_recv, gy_send, ga_recv, ga_send,
    zx_recv, zx_send, zy_recv, zy_send, ty_recv, tx_recv, t_send, sq_recv, sq_send,
):
    f, t = lax.axis_index("fsdp"), lax.axis_index("tensor")
    x, y = f // NY, f % NY
    z, c = t // 2, t % 2
    other = 1 - c

    def at_y(d):
        return (x * NY + (y + d) % NY, t)

    def at_x(d):
        return (((x + d) % NX) * NY + y, t)

    def at_z(d):
        return (f, ((z + d) % NZ) * 2 + c)

    sibling = (f, z * 2 + other)

    def send(src, dst, send_sem, recv_sem, device):
        pltpu.make_async_remote_copy(
            src_ref=src, dst_ref=dst, send_sem=send_sem, recv_sem=recv_sem, device_id=device, device_id_type=MESH
        ).start()

    def wait(ref, sem):
        pltpu.make_async_copy(ref, ref, sem).wait()

    load = pltpu.make_async_copy(momentum_hbm, momentum, load_sem)
    load.start()
    barrier = pltpu.get_barrier_semaphore()
    everyone = [at_y(d) for d in range(1, NY)] + [at_x(d) for d in range(1, NX)]
    everyone += [(f, (t + d) % (2 * NZ)) for d in range(1, 2 * NZ)]
    everyone += [(((x + d) % NX) * NY + y, z * 2 + other) for d in range(1, NX)]
    for device in everyone:
        pl.semaphore_signal(barrier, inc=1, device_id=device, device_id_type=MESH)

    stage[...] = jnp.zeros_like(stage)
    for q in range(4):
        width = min(512, COLS - 512 * q)
        stage[4 * q : 4 * q + 4, :width] = basis[:, 512 * q : 512 * q + width]
    slots[f] = stage[...].astype(BF16)
    pl.semaphore_wait(barrier, len(everyone))

    for d in range(1, NY):
        send(slots.at[f], slots.at[f], slot_send, slot_y_recv.at[d], at_y(d))
    for d in range(1, NX):
        send(slots.at[f], slots.at[f], slot_send, slot_x_recv.at[d], at_x(d))
    for e in range(1, NY):
        source = x * NY + (y - e) % NY
        wait(slots.at[source], slot_y_recv.at[e])
        for d in range(1, NX):
            send(slots.at[source], slots.at[source], slot_send, slot_x_recv.at[d], at_x(d))
    load.wait()
    for d in range(1, NX):
        group = slots.at[pl.ds(((x - d) % NX) * NY, NY)]
        wait(group, slot_x_recv.at[d])

    flat = slots[...].reshape(512, 512)
    to_row = lax.broadcasted_iota(jnp.int32, (RANK, 512), 0)
    from_row = lax.broadcasted_iota(jnp.int32, (RANK, 512), 1)
    total = None
    for q in range(4):
        width = min(512, COLS - 512 * q)
        pick = (from_row == (to_row // 4) * 16 + 4 * q + to_row % 4).astype(F32).astype(BF16)
        part = jnp.dot(pick, flat[:, :width], preferred_element_type=F32).astype(BF16)
        term = lax.dot_general(
            momentum[:, 512 * q : 512 * q + width], part, (((1,), (1,)), ((), ())), preferred_element_type=F32
        )
        total = term if total is None else total + term
    partial_buf[...] = total.reshape(2, ROWS // 2, RANK)

    send(partial_buf.at[other], pair_in, pair_send, pair_recv, sibling)
    wait(pair_in, pair_recv)
    wait(pair_in, pair_send)
    partial_buf[c] = partial_buf[c] + pair_in[...]
    for d in range(1, NZ):
        send(partial_buf.at[c, pl.ds(((z + d) % NZ) * 16, 16)], sum_in.at[d - 1], sum_send, sum_recv, at_z(d))
    wait(sum_in, sum_recv)
    total = partial_buf[c, pl.ds(z * 16, 16), :]
    for d in range(NZ - 1):
        total = total + sum_in[d]
    projected[c, z] = total
    for d in range(1, NZ):
        send(projected.at[c, z], projected.at[c, z], own_send, own_recv.at[d], at_z(d))
    for d in range(1, NZ):
        wait(projected.at[c, (z - d) % NZ], own_recv.at[d])
    send(projected.at[c], projected.at[c], half_send, half_recv, sibling)
    wait(projected.at[other], half_recv)

    proj = projected[...].reshape(ROWS, RANK)
    gram = lax.dot_general(proj, proj, (((0,), (0,)), ((), ())), precision=HIGH, preferred_element_type=F32)
    gram_buf[...] = gram.reshape(8, 16, RANK)
    for d in range(1, NX):
        send(gram_buf.at[2 * ((x + d) % NX) + c], gram_x.at[d - 1], gx_send, gx_recv, at_x(d))

    hi = proj.astype(BF16)
    left = proj - hi.astype(F32)
    mid = left.astype(BF16)
    low = (left - mid.astype(F32)).astype(BF16)
    for piece in range(NX):
        rows = None
        for term in (hi, mid, low):
            product = lax.dot_general(
                momentum[...][:, QUARTER * piece : QUARTER * (piece + 1)], term, (((0,), (0,)), ((), ())),
                preferred_element_type=F32,
            )
            rows = product if rows is None else rows + product
        zq[piece] = rows
    for d in range(1, NX):
        send(zq.at[(x + d) % NX], zx.at[d - 1], zx_send, zx_recv, at_x(d))

    wait(gram_x, gx_recv)
    own = 2 * x + c
    gram_mid[...] = gram_buf[own] + gram_x[0] + gram_x[1] + gram_x[2]
    for d in range(1, NY):
        send(gram_mid, gram_y.at[d - 1], gy_send, gy_recv, at_y(d))
    wait(gram_y, gy_recv)
    total = gram_mid[...]
    for d in range(NY - 1):
        total = total + gram_y[d]
    gram_full[own] = total
    for d in range(NX):
        for core in (c, other):
            if d == 0 and core is c:
                continue
            device = (((x + d) % NX) * NY + y, z * 2 + core)
            send(gram_full.at[own], gram_full.at[own], ga_send, ga_recv, device)
    wait(zx, zx_recv)
    zmid[pl.ds(0, QUARTER), :] = zq[x] + zx[0] + zx[1] + zx[2]
    zmid[pl.ds(QUARTER, NY * SLOT - QUARTER), :] = jnp.zeros((NY * SLOT - QUARTER, RANK), F32)
    for d in range(1, NY):
        send(zmid.at[pl.ds(((y + d) % NY) * SLOT, SLOT)], zy.at[d - 1], zy_send, zy_recv, at_y(d))
    wait(gram_full.at[pl.ds(0, 7)], ga_recv)

    inverse = inverse_factor(gram_full[...].reshape(RANK, RANK))
    ortho = lax.dot_general(proj, inverse, (((1,), (1,)), ((), ())), precision=HIGH, preferred_element_type=F32)
    ortho_out[...] = ortho.astype(BF16)

    wait(zy, zy_recv)
    total = zmid[pl.ds(y * SLOT, SLOT), :]
    for d in range(NY - 1):
        total = total + zy[d]
    mine = lax.dot_general(total, inverse, (((1,), (1,)), ((), ())), precision=HIGH, preferred_element_type=F32)
    back[x, y] = mine.astype(BF16)
    for d in range(1, NY):
        send(back.at[x, y], back.at[x, y], t_send, ty_recv.at[d], at_y(d))
    for d in range(1, NX):
        send(back.at[x, y], back.at[x, y], t_send, tx_recv.at[d], at_x(d))
    for e in range(1, NY):
        source = (y - e) % NY
        wait(back.at[x, source], ty_recv.at[e])
        for d in range(1, NX):
            send(back.at[x, source], back.at[x, source], t_send, tx_recv.at[d], at_x(d))
    for d in range(1, NX):
        wait(back.at[(x - d) % NX], tx_recv.at[d])

    squares = jnp.zeros((8, RANK), F32)
    for piece in range(NX):
        block = back[piece].reshape(NY * SLOT, RANK)[:QUARTER, :]
        back_out[QUARTER * piece : QUARTER * (piece + 1), :] = block
        block = block.astype(F32)
        squares = squares + jnp.sum((block * block).reshape(QUARTER // 8, 8, RANK), axis=0)
    sq_mine[...] = squares
    for d in range(1, 2 * NZ):
        send(sq_mine, sq_in.at[d - 1], sq_send, sq_recv, (f, (t + d) % (2 * NZ)))
    wait(sq_in, sq_recv)
    squares = sq_mine[...] + jnp.sum(sq_in[...], axis=0)
    squares = jnp.sum(squares, axis=0, keepdims=True)
    scale_out[...] = jnp.broadcast_to(lax.rsqrt(squares / FW + 1e-06), (8, RANK))

    wait(slots.at[pl.ds(0, 31)], slot_send)
    wait(sum_in, sum_send)
    wait(sum_in, own_send)
    wait(projected.at[c], half_send)
    wait(gram_x, gx_send)
    wait(gram_y, gy_send)
    wait(gram_full.at[pl.ds(0, 7)], ga_send)
    wait(zx, zx_send)
    wait(zy, zy_send)
    wait(slots.at[pl.ds(0, 31)], t_send)
    wait(sq_in, sq_send)


def update_kernel(momentum, weights, ortho, back, scale, weights_out, momentum_out, basis_out, basis_half):
    f = lax.axis_index("fsdp")

    @pl.when(pl.program_id(0) == 0)
    def _():
        full = back[...].astype(F32) * scale[0:1, :]
        basis_half[...] = full.astype(BF16)
        row = lax.broadcasted_iota(jnp.int32, (8, RANK), 0)
        col = lax.broadcasted_iota(jnp.int32, (8, RANK), 1)
        pick = (col == row + 4 * f).astype(F32)
        own = lax.dot_general(pick, full, (((1,), (1,)), ((), ())), precision=HIGH, preferred_element_type=F32)
        basis_out[...] = own[:4, :]

    q = ortho[...]
    feedback = lax.dot_general(q, back[...], (((1,), (1,)), ((), ())), preferred_element_type=F32)
    momentum_out[...] = (momentum[...].astype(F32) - 0.05 * feedback).astype(BF16)
    update = lax.dot_general(q, basis_half[...], (((1,), (1,)), ((), ())), preferred_element_type=F32)
    weights_out[...] = weights[...] - 0.02 * math.sqrt(DW / RANK) * update


def shards(momentum, weights, basis):
    vmem = pl.BlockSpec(memory_space=pltpu.VMEM)
    dma = pltpu.SemaphoreType.DMA
    ortho, back, scale = pl.pallas_call(
        exchange_kernel,
        out_shape=(
            jax.ShapeDtypeStruct((ROWS, RANK), BF16),
            jax.ShapeDtypeStruct((COLS, RANK), BF16),
            jax.ShapeDtypeStruct((8, RANK), F32),
        ),
        in_specs=[pl.BlockSpec(memory_space=pl.ANY), vmem],
        out_specs=(vmem, vmem, vmem),
        scratch_shapes=[
            pltpu.VMEM((ROWS, COLS), BF16),
            pltpu.VMEM((16, 512), F32),
            pltpu.VMEM((32, 16, 512), BF16),
            pltpu.VMEM((2, ROWS // 2, RANK), F32),
            pltpu.VMEM((ROWS // 2, RANK), F32),
            pltpu.VMEM((NZ - 1, 16, RANK), F32),
            pltpu.VMEM((2, NZ, 16, RANK), F32),
            pltpu.VMEM((8, 16, RANK), F32),
            pltpu.VMEM((NX - 1, 16, RANK), F32),
            pltpu.VMEM((16, RANK), F32),
            pltpu.VMEM((NY - 1, 16, RANK), F32),
            pltpu.VMEM((8, 16, RANK), F32),
            pltpu.VMEM((NX, QUARTER, RANK), F32),
            pltpu.VMEM((NX - 1, QUARTER, RANK), F32),
            pltpu.VMEM((NY * SLOT, RANK), F32),
            pltpu.VMEM((NY - 1, SLOT, RANK), F32),
            pltpu.VMEM((NX, NY, SLOT, RANK), BF16),
            pltpu.VMEM((8, RANK), F32),
            pltpu.VMEM((2 * NZ - 1, 8, RANK), F32),
            dma(()), dma((NY,)), dma((NX,)), dma(()), dma(()), dma(()), dma(()), dma(()),
            dma((NZ,)), dma(()), dma(()), dma(()), dma(()), dma(()), dma(()), dma(()), dma(()), dma(()),
            dma(()), dma(()), dma(()), dma(()), dma((NY,)), dma((NX,)), dma(()), dma(()), dma(()),
        ],
        compiler_params=pltpu.CompilerParams(
            collective_id=0, has_side_effects=True, vmem_limit_bytes=40 * 2**20
        ),
        name="exchange",
    )(momentum, basis.T)
    steps = 4
    block = ROWS // steps
    weights_out, momentum_out, basis_out = pl.pallas_call(
        update_kernel,
        grid=(steps,),
        out_shape=(
            jax.ShapeDtypeStruct((ROWS, COLS), F32),
            jax.ShapeDtypeStruct((ROWS, COLS), BF16),
            jax.ShapeDtypeStruct((4, COLS), F32),
        ),
        in_specs=[
            pl.BlockSpec((block, COLS), lambda i: (i, 0)),
            pl.BlockSpec((block, COLS), lambda i: (i, 0)),
            pl.BlockSpec((block, RANK), lambda i: (i, 0)),
            vmem,
            vmem,
        ],
        out_specs=(
            pl.BlockSpec((block, COLS), lambda i: (i, 0)),
            pl.BlockSpec((block, COLS), lambda i: (i, 0)),
            pl.BlockSpec((4, COLS), lambda i: (0, 0)),
        ),
        scratch_shapes=[pltpu.VMEM((COLS, RANK), BF16)],
        compiler_params=pltpu.CompilerParams(vmem_limit_bytes=40 * 2**20),
        name="update",
    )(momentum, weights, ortho, back, scale)
    return weights_out, momentum_out, basis_out.T


def solution(mesh):
    in_specs = (P("fsdp", "tensor"), P("fsdp", "tensor"), P("tensor", "fsdp"))
    out_specs = (P("fsdp", "tensor"), P("fsdp", "tensor"), P("tensor", "fsdp"))
    return jax.shard_map(shards, mesh=mesh, in_specs=in_specs, out_specs=out_specs, check_vma=False)
```

time: 554 us -> 86.8 us (0.16)
  waiting for transfers between devices: 432 us -> 0 us
  Pallas kernels: 0 us -> 82.6 us
  blocking collectives: 68.3 us -> 0 us
  other arithmetic: 27 us -> 0 us
  between operations: 13.8 us -> 0.66 us
  matrix products: 11.1 us -> 0 us
    psum x3 -> x0, waiting for transfers between devices: 432 us -> none  [the longest x1 156 us: shards(): lax.psum(local_back.astype(jnp.bfloat16), 'fsdp').astype(jnp.float32)]
    pallas_call x0 -> x2, Pallas kernels: none -> 82.6 us  [the longest x1 78.9 us: shards(): pl.pallas_call(exchange_kernel, out_shape=(jax.ShapeDtypeStruct((ROWS, RA...]
    all_gather x1 -> x0, blocking collectives: 39.4 us -> none  [shards(): lax.all_gather(basis_half, 'fsdp', axis=1, tiled=True)]
    psum x1 -> x0, blocking collectives: 28.9 us -> none  [shards(): squares = lax.psum(jnp.sum(transposed * transposed, axis=0), 'tensor')]
    another operation x5 -> x0, other arithmetic: 22.9 us -> none  [the longest x3 12.4 us: orthonormalize(): factor = jnp.linalg.cholesky(gram_matrix)]
    dot_general x5 -> x0, matrix products: 9.91 us -> none  [the longest x1 2.8 us: shards(): lax.dot_general(ortho, full_basis, (((1,), (1,)), ((), ())), precision=HIGH)]
  transfers between devices with their start and end apart: 3 -> 0, of which waited for: 3 -> 0; matrix products, arithmetic and copies ran while one was open for 0% -> 0% of each run, Pallas kernels for 0% -> 0%
where the time goes in v1:
time: 86.8 us; the launch traced here: 86.6 us
  Pallas kernels  82.6 us (95%)
  local copies, waits for them, and re-layouts  3.34 us (4%)
    pallas_call x1, Pallas kernels, shards(): pl.pallas_call(exchange_kernel, out_shape=(jax.ShapeDtypeStruct((ROWS, RA...  78.9 us
    pallas_call x1, Pallas kernels, shards(): pl.pallas_call(update_kernel, grid=(steps,), out_shape=(jax.ShapeDtypeStr...  3.69 us
    unnamed x6, local copies, waits for them, and re-layouts  3.34 us

profile of v1, /device:TPU:1, one launch (start us, length us, event | category | flops | bytes accessed | tf_op | source)
XLA Modules:
  0.0 86.6 jit_solution(17410989329810743087)
XLA Ops:
  0.6 0.0 copy-start
  0.6 1.1 %copy-done = bf16[256,1664]{1,0:T(8,128)(2,1)S(1)} copy-done((bf16[256,1664]{1,0:T(8,128)(2,1)S(1)}, bf16[256,1664]{1,0:T(8,128)(2,1)}, u32[]{:S(2)}) %copy-start) | copy-done | bytes 851992
  1.8 0.0 copy-start.2
  1.8 0.7 copy-done.2
  2.5 78.9 %exchange.1 = (bf16[256,128]{1,0:T(8,128)(2,1)S(1)}, bf16[1664,128]{1,0:T(8,128)(2,1)S(1)}, f32[8,128]{1,0:T(8,128)S(1)}) custom-call(bf16[256,1664]{1,0:T(8,128)(2,1)S(1)} %copy-done, f32[4,1664]{1,0:T(4,128)S(1)} %bitcast.2), custom_call_target="tpu_custom_call" | custom-call | tf_op jit(solution)/shard_map/exchange/pallas_call | solution.py:268
  81.4 0.0 copy-start.1
  81.4 1.4 %copy-done.1 = f32[256,1664]{1,0:T(8,128)S(1)} copy-done((f32[256,1664]{1,0:T(8,128)S(1)}, f32[256,1664]{1,0:T(8,128)}, u32[]{:S(2)}) %copy-start.1) | copy-done | bytes 1703960
  82.9 3.7 %update.1 = (f32[256,1664]{1,0:T(8,128)}, bf16[256,1664]{1,0:T(8,128)(2,1)}, f32[4,1664]{1,0:T(4,128)}) custom-call(bf16[256,1664]{1,0:T(8,128)(2,1)S(1)} %copy-done, f32[256,1664]{1,0:T(8,128)S(1)} %copy-done.1, bf16[256,128]{1,0:T(8,128)(2,1)S(1)} %get-tuple-element.9.ortho, bf16[1664,128]{1,0:T(8,128)(2,1)S(1)} %get-tuple-element.10.back, ...), custom_call_target="tpu_custom_call" | custom-call | tf_op jit(solution)/shard_map/update/pallas_call | solution.py:308
Async XLA Ops:
  0.6 1.2 %copy-start = (bf16[256,1664]{1,0:T(8,128)(2,1)S(1)}, bf16[256,1664]{1,0:T(8,128)(2,1)}, u32[]{:S(2)}) copy-start(bf16[256,1664]{1,0:T(8,128)(2,1)} %momentum.1) | copy-start | bytes 2555908
  1.8 0.7 copy-start.2
  81.4 1.5 %copy-start.1 = (f32[256,1664]{1,0:T(8,128)S(1)}, f32[256,1664]{1,0:T(8,128)}, u32[]{:S(2)}) copy-start(f32[256,1664]{1,0:T(8,128)} %weights.1) | copy-start | bytes 5111812

commit v2 on v1

v2 whole, which is shorter than its diff:
```python
import functools
import math

import jax
import jax.numpy as jnp
from jax import lax
from jax.experimental import pallas as pl
from jax.experimental.pallas import tpu as pltpu
from jax.sharding import PartitionSpec as P

DW = 8192
FW = 26624
RANK = 128
ROWS = 256
COLS = 1664
NX, NY, NZ = 4, 8, 8
QUARTER = COLS // NX
SLOT = 64
NSLOT = 7
FAR_FIRST = (4, 3, 5, 2, 6, 1, 7)
NEAR_FIRST = (1, 7, 2, 6, 3, 5, 4)

HIGH = lax.Precision.HIGHEST
ACROSS = (((1,), (1,)), ((), ()))
MESH = pl.DeviceIdType.MESH
F32 = jnp.float32
BF16 = jnp.bfloat16


def spread_row(a, k):
    return jnp.broadcast_to(a[k : k + 1, :], a.shape)


def inverse_factor(gram, between):
    lane = lax.broadcasted_iota(jnp.int32, (8, RANK), 1)
    sub = lax.broadcasted_iota(jnp.int32, (8, RANK), 0)
    lanes = lax.broadcasted_iota(jnp.int32, (RANK, RANK), 1)
    rows, coming, rest = gram[0:8], gram[8:16], gram[16:]
    done = []
    for first in range(0, RANK, 8):
        last = first + 8
        more = last < RANK
        inside = (lane >= first) & (lane < last)
        block = [jnp.broadcast_to(rows[:, first + k : first + k + 1], (8, RANK)) for k in range(8)]
        rows = jnp.where(inside, jnp.where(lane - first == sub, 1.0, 0.0), rows)
        if more:
            below = [jnp.broadcast_to(coming[:, first + k : first + k + 1], (8, RANK)) for k in range(8)]
            coming = jnp.where(inside, 0.0, coming)
        pivots = None
        for k in range(8):
            pivot = spread_row(block[k], k)
            inv = 1.0 / pivot
            pivots = pivot if pivots is None else jnp.where(sub == k, pivot, pivots)
            row = spread_row(rows, k)
            mult = jnp.where(sub > k, block[k] * inv, 0.0)
            if more:
                mult_below = below[k] * inv
                coming = coming - mult_below * row
            for n in range(k + 1, 8):
                entry = spread_row(block[n], k)
                block[n] = block[n] - mult * entry
                if more:
                    below[n] = below[n] - mult_below * entry
            rows = rows - mult * row
        rows = rows * lax.rsqrt(pivots)
        done.append(jnp.where(lane < last, rows, 0.0))
        if last + 8 < RANK:
            upper = jnp.where(lane >= last + 8, rows, 0.0)
            base = jnp.where((lanes[last + 8 :] >= first) & (lanes[last + 8 :] < last), 0.0, rest)
            change = lax.dot_general(upper, rows, (((0,), (0,)), ((), ())), precision=HIGH, preferred_element_type=F32)
            rest = base - change[last + 8 :, :]
            rows, coming, rest = coming, rest[:8], rest[8:]
        else:
            rows = coming
        if first // 8 in between:
            between[first // 8]()
    return jnp.concatenate(done, axis=0)


def exchange_kernel(
    momentum_hbm, weights_hbm, basis_hbm, weights_out, momentum_out, basis_out,
    momentum, weights, basis, stage, slots, partial, pair_in, sum_in, projected, gram_buf, gram_x, gram_mid, gram_y, gram_full,
    zq, zx, zmid, zy, back, whole, sq_t, sq_f, sq_t_in, sq_f_in,
    load_sem, weights_sem, basis_sem, slot_y_recv, slot_x_recv, slot_send, pair_recv, pair_send, sum_recv, sum_send,
    own_recv, own_send, half_recv, half_send, gx_recv, gx_send, gy_recv, gy_send, ga_recv, ga_send,
    zx_recv, zx_send, zy_recv, zy_send, ty_recv, tx_recv, t_send, sq_recv, sq_send,
):
    f, t = lax.axis_index("fsdp"), lax.axis_index("tensor")
    x, y = f // NY, f % NY
    z, c = t // 2, t % 2
    other = 1 - c
    pending = []

    def at_y(d):
        return (x * NY + (y + d) % NY, t)

    def at_x(d):
        return (((x + d) % NX) * NY + y, t)

    def at_z(d):
        return (f, ((z + d) % NZ) * 2 + c)

    sibling = (f, z * 2 + other)

    def send(src, dst, send_sem, recv_sem, device):
        pltpu.make_async_remote_copy(
            src_ref=src, dst_ref=dst, send_sem=send_sem, recv_sem=recv_sem, device_id=device, device_id_type=MESH
        ).start()

    def wait(ref, sem):
        pltpu.make_async_copy(ref, ref, sem).wait()

    def later(ref, sem, needed=None):
        pending.append((ref, sem, needed))

    def flush():
        for ref, sem, needed in pending:
            if needed is None:
                wait(ref, sem)
            else:
                pl.when(needed)(functools.partial(wait, ref, sem))

    basis_load = pltpu.make_async_copy(basis_hbm, basis, basis_sem)
    basis_load.start()
    load = pltpu.make_async_copy(momentum_hbm, momentum, load_sem)
    load.start()
    weights_load = pltpu.make_async_copy(weights_hbm, weights, weights_sem)
    weights_load.start()
    barrier = pltpu.get_barrier_semaphore()
    everyone = [at_y(d) for d in range(1, NY)] + [at_x(d) for d in range(1, NX)]
    everyone += [at_z(d) for d in range(1, NZ)] + [sibling]
    for device in everyone:
        pl.semaphore_signal(barrier, inc=1, device_id=device, device_id_type=MESH)

    stage[...] = jnp.zeros_like(stage)
    basis_load.wait()
    for q in range(4):
        width = min(512, COLS - 512 * q)
        stage[4 * q : 4 * q + 4, :width] = basis[:, 512 * q : 512 * q + width]
    slots[f] = stage[...].astype(BF16)
    load.wait()
    weights_load.wait()
    pl.semaphore_wait(barrier, len(everyone))

    for d in FAR_FIRST:
        send(slots.at[f], slots.at[f], slot_send, slot_y_recv.at[d], at_y(d))
    for d in (2, 1, 3):
        send(slots.at[f], slots.at[f], slot_send, slot_x_recv.at[d], at_x(d))
    for e in NEAR_FIRST:
        source = x * NY + (y - e) % NY
        wait(slots.at[source], slot_y_recv.at[e])
        for d in (2, 1, 3):
            send(slots.at[source], slots.at[source], slot_send, slot_x_recv.at[d], at_x(d))
    later(slots.at[pl.ds(0, 31)], slot_send)
    for d in range(1, NX):
        wait(slots.at[pl.ds(((x - d) % NX) * NY, NY)], slot_x_recv.at[d])

    flat = slots[...].reshape(512, 512)
    to_row = lax.broadcasted_iota(jnp.int32, (RANK, 512), 0)
    from_row = lax.broadcasted_iota(jnp.int32, (RANK, 512), 1)
    parts = []
    for q in range(4):
        width = min(512, COLS - 512 * q)
        pick = (from_row == (to_row // 4) * 16 + 4 * q + to_row % 4).astype(F32).astype(BF16)
        parts.append(jnp.dot(pick, flat[:, :width], preferred_element_type=F32).astype(BF16))

    def product(half):
        total = None
        for q in range(4):
            width = min(512, COLS - 512 * q)
            block = momentum[pl.ds(half * (ROWS // 2), ROWS // 2), 512 * q : 512 * q + width]
            term = lax.dot_general(block, parts[q], (((1,), (1,)), ((), ())), preferred_element_type=F32)
            total = term if total is None else total + term
        return total

    partial[other] = product(other)
    for e in FAR_FIRST + (0,):
        rows = pl.ds(((z + e) % NZ) * 16, 16)
        send(partial.at[other, rows], pair_in.at[rows], pair_send, pair_recv.at[e], sibling)
    later(pair_in, pair_send)
    partial[c] = product(c)
    for e in FAR_FIRST:
        rows = pl.ds(((z + e) % NZ) * 16, 16)
        wait(pair_in.at[rows], pair_recv.at[e])
        partial[c, rows, :] = partial[c, rows, :] + pair_in[rows, :]
        send(partial.at[c, rows], sum_in.at[e - 1], sum_send, sum_recv, at_z(e))
    later(sum_in, sum_send)
    rows = pl.ds(z * 16, 16)
    wait(pair_in.at[rows], pair_recv.at[0])
    total = partial[c, rows, :] + pair_in[rows, :]
    wait(sum_in, sum_recv)
    for d in range(NZ - 1):
        total = total + sum_in[d]
    projected[c, z] = total
    for d in FAR_FIRST:
        send(projected.at[c, z], projected.at[c, z], own_send, own_recv.at[d], at_z(d))
    later(sum_in, own_send)
    send(projected.at[c, z], projected.at[c, z], half_send, half_recv, sibling)
    for d in NEAR_FIRST:
        source = (z - d) % NZ
        wait(projected.at[c, source], own_recv.at[d])
        send(projected.at[c, source], projected.at[c, source], half_send, half_recv, sibling)
    wait(projected.at[other], half_recv)
    later(projected.at[c], half_send)

    proj = projected[...].reshape(ROWS, RANK)
    gram = lax.dot_general(proj, proj, (((0,), (0,)), ((), ())), precision=HIGH, preferred_element_type=F32)
    gram_buf[...] = gram.reshape(8, 16, RANK)
    for d in range(1, NX):
        send(gram_buf.at[2 * ((x + d) % NX) + c], gram_x.at[d - 1], gx_send, gx_recv, at_x(d))
    later(gram_x, gx_send)

    hi = proj.astype(BF16)
    left = proj - hi.astype(F32)
    mid = left.astype(BF16)
    low = (left - mid.astype(F32)).astype(BF16)
    terms = jnp.concatenate([hi, mid, low], axis=1)
    for piece in range(NX):
        out = lax.dot_general(
            momentum[:, QUARTER * piece : QUARTER * (piece + 1)], terms, (((0,), (0,)), ((), ())),
            preferred_element_type=F32,
        )
        out = out[:, :RANK] + out[:, RANK : 2 * RANK] + out[:, 2 * RANK :]
        for n in range(NSLOT):
            zq[piece, n, : min(SLOT, QUARTER - n * SLOT), :] = out[n * SLOT : (n + 1) * SLOT, :]
        zq[piece, NSLOT - 1, QUARTER - (NSLOT - 1) * SLOT :, :] = jnp.zeros((NSLOT * SLOT - QUARTER, RANK), F32)

    def send_slot(e):
        slot = (y + e) % NY

        @pl.when(slot < NSLOT)
        def _():
            for d in (2, 1, 3):
                send(zq.at[(x + d) % NX, slot], zx.at[x, slot], zx_send, zx_recv.at[e], at_x(d))

    def reduce_slot(e):
        slot = (y + e) % NY

        @pl.when(slot < NSLOT)
        def _():
            wait(zx.at[pl.ds(0, 3), 0], zx_recv.at[e])
            total = zq[x, slot]
            for d in range(1, NX):
                total = total + zx[(x + d) % NX, slot]
            zmid[slot] = total
            if e:
                send(zmid.at[slot], zy.at[e - 1], zy_send.at[e], zy_recv, at_y(e))

        if e:
            later(zmid.at[0], zy_send.at[e], slot < NSLOT)

    slot_order = FAR_FIRST + (0,)
    for e in slot_order:
        send_slot(e)
    later(zx.at[pl.ds(0, 3)], zx_send)

    wait(gram_x, gx_recv)
    own = 2 * x + c
    gram_mid[...] = gram_buf[own] + gram_x[0] + gram_x[1] + gram_x[2]
    for d in FAR_FIRST:
        send(gram_mid, gram_y.at[d - 1], gy_send, gy_recv, at_y(d))
    later(gram_y, gy_send)
    for e in slot_order[:2]:
        reduce_slot(e)
    wait(gram_y, gy_recv)
    total = gram_mid[...]
    for d in range(NY - 1):
        total = total + gram_y[d]
    gram_full[own] = total
    for d in (2, 1, 3, 0):
        for core in (other, c):
            if d == 0 and core is c:
                continue
            device = (((x + d) % NX) * NY + y, z * 2 + core)
            send(gram_full.at[own], gram_full.at[own], ga_send, ga_recv, device)
    later(gram_full.at[pl.ds(0, 7)], ga_send)
    for e in slot_order[2:5]:
        reduce_slot(e)
    wait(gram_full.at[pl.ds(0, 7)], ga_recv)

    between = {5: functools.partial(reduce_slot, slot_order[5]), 8: functools.partial(reduce_slot, slot_order[6])}
    inverse = inverse_factor(gram_full[...].reshape(RANK, RANK), between)
    reduce_slot(0)
    holder = y < NSLOT

    @pl.when(holder)
    def _():
        wait(zy, zy_recv)
        total = zmid[y]
        for d in range(NY - 1):
            total = total + zy[d]
        mine = lax.dot_general(total, inverse, (((1,), (1,)), ((), ())), precision=HIGH, preferred_element_type=F32)
        mine = mine.astype(BF16)
        back[x, y] = mine
        for d in FAR_FIRST:
            send(back.at[x, y], back.at[x, y], t_send.at[0], ty_recv.at[d], at_y(d))
        for d in (2, 1, 3):
            send(back.at[x, y], back.at[x, y], t_send.at[0], tx_recv.at[d], at_x(d))
        mine = mine.astype(F32)
        sq_t[...] = jnp.sum(mine * mine, axis=0, keepdims=True)

    @pl.when(jnp.logical_not(holder))
    def _():
        sq_t[...] = jnp.zeros_like(sq_t)

    for d in range(1, 2 * NZ):
        send(sq_t, sq_t_in.at[d - 1], sq_send.at[0], sq_recv.at[0], (f, (t + d) % (2 * NZ)))
    later(sq_t_in, sq_send.at[0])
    ortho = lax.dot_general(proj, inverse, (((1,), (1,)), ((), ())), precision=HIGH, preferred_element_type=F32)

    def relay(e):
        source = (y - e) % NY

        @pl.when(source < NSLOT)
        def _():
            wait(back.at[x, source], ty_recv.at[e])
            for d in (2, 1, 3):
                send(back.at[x, source], back.at[x, source], t_send.at[1], tx_recv.at[d], at_x(d))

    for e in NEAR_FIRST[:6]:
        relay(e)
    wait(sq_t_in, sq_recv.at[0])
    sq_f[...] = sq_t[...] + jnp.sum(sq_t_in[...], axis=0)
    for dy in FAR_FIRST + (0,):
        for dx in (2, 1, 3, 0):
            if dx or dy:
                device = (((x + dx) % NX) * NY + (y + dy) % NY, t)
                send(sq_f, sq_f_in.at[dx * NY + dy - 1], sq_send.at[1], sq_recv.at[1], device)
    later(sq_f_in, sq_send.at[1])
    relay(NEAR_FIRST[6])
    later(slots.at[pl.ds(0, 10)], t_send.at[0], holder)
    later(slots.at[pl.ds(0, 18)], t_send.at[1], holder)
    later(slots.at[pl.ds(0, 21)], t_send.at[1], jnp.logical_not(holder))
    def gathered(d):
        piece = (x - d) % NX
        if d:
            wait(back.at[piece], tx_recv.at[d])
        whole[pl.ds(pl.multiple_of(piece * QUARTER, 32), QUARTER), :] = back[piece].reshape(NSLOT * SLOT, RANK)[:QUARTER, :]

    for d in (0, 1, 3, 2):
        gathered(d)
    feedback = lax.dot_general(ortho.astype(BF16), whole[...], ACROSS, preferred_element_type=F32)
    momentum_out[...] = (momentum[...].astype(F32) - 0.05 * feedback).astype(BF16)
    wait(sq_f_in, sq_recv.at[1])
    squares = sq_f[...] + jnp.sum(sq_f_in[...], axis=0)
    scale = lax.rsqrt(squares / FW + 1e-06)
    row = lax.broadcasted_iota(jnp.int32, (16, RANK), 0)
    col = lax.broadcasted_iota(jnp.int32, (16, RANK), 1)
    pick = (col == row + 4 * f) & (row < 4)
    left = jnp.concatenate([ortho * scale, pick.astype(F32)], axis=0).astype(BF16)
    result = lax.dot_general(left, whole[...], ACROSS, preferred_element_type=F32)
    weights_out[...] = weights[...] - 0.02 * math.sqrt(DW / RANK) * result[:ROWS]
    basis_out[...] = result[ROWS : ROWS + 4] * jnp.sum(jnp.where(pick, scale, 0.0), axis=1, keepdims=True)[:4]
    flush()


def place_kernel(weights, momentum, basis, weights_out, momentum_out, basis_out, sems):
    copies = [
        pltpu.make_async_copy(source, target, sems.at[i])
        for i, (source, target) in enumerate(((weights, weights_out), (momentum, momentum_out), (basis, basis_out)))
    ]
    for copy in copies:
        copy.start()
    for copy in copies:
        copy.wait()


def shards(momentum, weights, basis):
    vmem = pl.BlockSpec(memory_space=pltpu.VMEM)
    hbm = pl.BlockSpec(memory_space=pltpu.HBM)
    dma = pltpu.SemaphoreType.DMA
    weights_out, momentum_out, basis_out = pl.pallas_call(
        exchange_kernel,
        out_shape=(
            jax.ShapeDtypeStruct((ROWS, COLS), F32),
            jax.ShapeDtypeStruct((ROWS, COLS), BF16),
            jax.ShapeDtypeStruct((4, COLS), F32),
        ),
        in_specs=[hbm, hbm, hbm],
        out_specs=(vmem, vmem, vmem),
        scratch_shapes=[
            pltpu.VMEM((ROWS, COLS), BF16),
            pltpu.VMEM((ROWS, COLS), F32),
            pltpu.VMEM((4, COLS), F32),
            pltpu.VMEM((16, 512), F32),
            pltpu.VMEM((32, 16, 512), BF16),
            pltpu.VMEM((2, ROWS // 2, RANK), F32),
            pltpu.VMEM((ROWS // 2, RANK), F32),
            pltpu.VMEM((NZ - 1, 16, RANK), F32),
            pltpu.VMEM((2, NZ, 16, RANK), F32),
            pltpu.VMEM((8, 16, RANK), F32),
            pltpu.VMEM((NX - 1, 16, RANK), F32),
            pltpu.VMEM((16, RANK), F32),
            pltpu.VMEM((NY - 1, 16, RANK), F32),
            pltpu.VMEM((8, 16, RANK), F32),
            pltpu.VMEM((NX, NSLOT, SLOT, RANK), F32),
            pltpu.VMEM((NX, NSLOT, SLOT, RANK), F32),
            pltpu.VMEM((NSLOT, SLOT, RANK), F32),
            pltpu.VMEM((NY - 1, SLOT, RANK), F32),
            pltpu.VMEM((NX, NSLOT, SLOT, RANK), BF16),
            pltpu.VMEM((COLS, RANK), BF16),
            pltpu.VMEM((1, RANK), F32),
            pltpu.VMEM((1, RANK), F32),
            pltpu.VMEM((2 * NZ - 1, 1, RANK), F32),
            pltpu.VMEM((NX * NY - 1, 1, RANK), F32),
            dma(()), dma(()), dma(()), dma((NY,)), dma((NX,)), dma(()), dma((NZ,)), dma(()), dma(()), dma(()),
            dma((NZ,)), dma(()), dma(()), dma(()), dma(()), dma(()), dma(()), dma(()), dma(()), dma(()),
            dma((NY,)), dma(()), dma(()), dma((NY,)), dma((NY,)), dma((NX,)), dma((2,)), dma((2,)), dma((2,)),
        ],
        compiler_params=pltpu.CompilerParams(
            collective_id=0, has_side_effects=True, vmem_limit_bytes=48 * 2**20
        ),
        name="exchange",
    )(*[pltpu.with_memory_space_constraint(a, pltpu.HBM) for a in (momentum, weights, basis.T)])
    weights_out, momentum_out, basis_out = pl.pallas_call(
        place_kernel,
        out_shape=(
            jax.ShapeDtypeStruct((ROWS, COLS), F32),
            jax.ShapeDtypeStruct((ROWS, COLS), BF16),
            jax.ShapeDtypeStruct((4, COLS), F32),
        ),
        in_specs=[pl.BlockSpec(memory_space=pl.ANY)] * 3,
        out_specs=(hbm, hbm, hbm),
        scratch_shapes=[dma((3,))],
        compiler_params=pltpu.CompilerParams(vmem_limit_bytes=2 * 2**20),
        name="place",
    )(weights_out, momentum_out, basis_out)
    return weights_out, momentum_out, basis_out.T


def solution(mesh):
    in_specs = (P("fsdp", "tensor"), P("fsdp", "tensor"), P("tensor", "fsdp"))
    out_specs = (P("fsdp", "tensor"), P("fsdp", "tensor"), P("tensor", "fsdp"))
    return jax.shard_map(shards, mesh=mesh, in_specs=in_specs, out_specs=out_specs, check_vma=False)
```

time: 86.8 us -> 71 us (0.82)
  Pallas kernels: 82.6 us -> 70.2 us
  local copies, waits for them, and re-layouts: 3.34 us -> 0 us
    pallas_call x2, Pallas kernels: 82.6 us -> 70.2 us  [the longest x1 68.7 us: shards(): pl.pallas_call(exchange_kernel, out_shape=(jax.ShapeDtypeStruct((ROWS, CO...]
    unnamed x6 -> x0, local copies, waits for them, and re-layouts: 3.34 us -> none
where the time goes in v2:
time: 71 us; the launch traced here: 70.9 us
  Pallas kernels  70.2 us (99%)
    pallas_call x1, Pallas kernels, shards(): pl.pallas_call(exchange_kernel, out_shape=(jax.ShapeDtypeStruct((ROWS, CO...  68.7 us
    pallas_call x1, Pallas kernels, shards(): pl.pallas_call(place_kernel, out_shape=(jax.ShapeDtypeStruct((ROWS, COLS)...  1.49 us

profile of v2, /device:TPU:1, one launch (start us, length us, event | category | flops | bytes accessed | tf_op | source)
XLA Modules:
  0.0 70.9 jit_solution(9758998896235260151)
XLA Ops:
  0.6 68.7 %exchange.1 = (f32[256,1664]{1,0:T(8,128)S(1)}, bf16[256,1664]{1,0:T(8,128)(2,1)S(1)}, f32[4,1664]{1,0:T(4,128)S(1)}) custom-call(bf16[256,1664]{1,0:T(8,128)(2,1)} %momentum_hbm.1, f32[256,1664]{1,0:T(8,128)} %weights_hbm.1, f32[4,1664]{1,0:T(4,128)} %bitcast.2), custom_call_target="tpu_custom_call" | custom-call | tf_op jit(solution)/shard_map/exchange/pallas_call | solution.py:372
  69.4 1.5 %place.1 = (f32[256,1664]{1,0:T(8,128)}, bf16[256,1664]{1,0:T(8,128)(2,1)}, f32[4,1664]{1,0:T(4,128)}) custom-call(f32[256,1664]{1,0:T(8,128)S(1)} %get-tuple-element.9.weights, bf16[256,1664]{1,0:T(8,128)(2,1)S(1)} %get-tuple-element.10.momentum, f32[4,1664]{1,0:T(4,128)S(1)} %get-tuple-element.11.basis), custom_call_target="tpu_custom_call" | custom-call | tf_op jit(solution)/shard_map/place/pallas_call | solution.py:415

commit v3 on v2

--- a/solution.py
+++ b/solution.py
@@ -16,6 +16,7 @@
 NX, NY, NZ = 4, 8, 8
 QUARTER = COLS // NX
 SLOT = 64
+AHEAD = 3
 NSLOT = 7
 FAR_FIRST = (4, 3, 5, 2, 6, 1, 7)
 NEAR_FIRST = (1, 7, 2, 6, 3, 5, 4)
@@ -31,21 +32,24 @@
     return jnp.broadcast_to(a[k : k + 1, :], a.shape)
 
 
-def inverse_factor(gram, between):
+def inverse_factor(gram):
     lane = lax.broadcasted_iota(jnp.int32, (8, RANK), 1)
     sub = lax.broadcasted_iota(jnp.int32, (8, RANK), 0)
     lanes = lax.broadcasted_iota(jnp.int32, (RANK, RANK), 1)
-    rows, coming, rest = gram[0:8], gram[8:16], gram[16:]
+    panels = [gram[8 * i : 8 * i + 8] for i in range(AHEAD + 1)]
+    rest = gram[8 * (AHEAD + 1) :]
     done = []
     for first in range(0, RANK, 8):
         last = first + 8
-        more = last < RANK
         inside = (lane >= first) & (lane < last)
-        block = [jnp.broadcast_to(rows[:, first + k : first + k + 1], (8, RANK)) for k in range(8)]
-        rows = jnp.where(inside, jnp.where(lane - first == sub, 1.0, 0.0), rows)
-        if more:
-            below = [jnp.broadcast_to(coming[:, first + k : first + k + 1], (8, RANK)) for k in range(8)]
-            coming = jnp.where(inside, 0.0, coming)
+
+        def columns(panel):
+            return [jnp.broadcast_to(panel[:, first + k : first + k + 1], (8, RANK)) for k in range(8)]
+
+        block = columns(panels[0])
+        below = [columns(panel) for panel in panels[1:]]
+        rows = jnp.where(inside, jnp.where(lane - first == sub, 1.0, 0.0), panels[0])
+        panels = [jnp.where(inside, 0.0, panel) for panel in panels[1:]]
         pivots = None
         for k in range(8):
             pivot = spread_row(block[k], k)
@@ -53,37 +57,35 @@
             pivots = pivot if pivots is None else jnp.where(sub == k, pivot, pivots)
             row = spread_row(rows, k)
             mult = jnp.where(sub > k, block[k] * inv, 0.0)
-            if more:
-                mult_below = below[k] * inv
-                coming = coming - mult_below * row
-            for n in range(k + 1, 8):
-                entry = spread_row(block[n], k)
-                block[n] = block[n] - mult * entry
-                if more:
-                    below[n] = below[n] - mult_below * entry
+            entries = {n: spread_row(block[n], k) for n in range(k + 1, 8)}
+            for n in entries:
+                block[n] = block[n] - mult * entries[n]
             rows = rows - mult * row
+            for i, column in enumerate(below):
+                mult = column[k] * inv
+                for n in entries:
+                    column[n] = column[n] - mult * entries[n]
+                panels[i] = panels[i] - mult * row
         rows = rows * lax.rsqrt(pivots)
         done.append(jnp.where(lane < last, rows, 0.0))
-        if last + 8 < RANK:
-            upper = jnp.where(lane >= last + 8, rows, 0.0)
-            base = jnp.where((lanes[last + 8 :] >= first) & (lanes[last + 8 :] < last), 0.0, rest)
+        start = last + 8 * AHEAD
+        if start < RANK:
+            upper = jnp.where(lane >= start, rows, 0.0)
+            base = jnp.where((lanes[start:] >= first) & (lanes[start:] < last), 0.0, rest)
             change = lax.dot_general(upper, rows, (((0,), (0,)), ((), ())), precision=HIGH, preferred_element_type=F32)
-            rest = base - change[last + 8 :, :]
-            rows, coming, rest = coming, rest[:8], rest[8:]
-        else:
-            rows = coming
-        if first // 8 in between:
-            between[first // 8]()
+            rest = base - change[start:, :]
+            panels.append(rest[:8])
+            rest = rest[8:]
     return jnp.concatenate(done, axis=0)
 
 
 def exchange_kernel(
     momentum_hbm, weights_hbm, basis_hbm, weights_out, momentum_out, basis_out,
-    momentum, weights, basis, stage, slots, partial, pair_in, sum_in, projected, gram_buf, gram_x, gram_mid, gram_y, gram_full,
-    zq, zx, zmid, zy, back, whole, sq_t, sq_f, sq_t_in, sq_f_in,
+    momentum, momentum_t, weights, basis, stage, slots, full_basis, partial, pair_in, sum_in, projected, gram_buf, gram_x, gram_mid, gram_y, gram_full,
+    zq, zfar, zx, zmid, zy, back, whole, sq_t, sq_f, sq_t_in, sq_f_in,
     load_sem, weights_sem, basis_sem, slot_y_recv, slot_x_recv, slot_send, pair_recv, pair_send, sum_recv, sum_send,
     own_recv, own_send, half_recv, half_send, gx_recv, gx_send, gy_recv, gy_send, ga_recv, ga_send,
-    zx_recv, zx_send, zy_recv, zy_send, ty_recv, tx_recv, t_send, sq_recv, sq_send,
+    zfar_recv, zx_recv, zx_send, zy_recv, zy_send, ty_recv, tx_recv, t_send, sq_recv, sq_send,
 ):
     f, t = lax.axis_index("fsdp"), lax.axis_index("tensor")
     x, y = f // NY, f % NY
@@ -122,15 +124,15 @@
 
     basis_load = pltpu.make_async_copy(basis_hbm, basis, basis_sem)
     basis_load.start()
-    load = pltpu.make_async_copy(momentum_hbm, momentum, load_sem)
-    load.start()
-    weights_load = pltpu.make_async_copy(weights_hbm, weights, weights_sem)
-    weights_load.start()
     barrier = pltpu.get_barrier_semaphore()
     everyone = [at_y(d) for d in range(1, NY)] + [at_x(d) for d in range(1, NX)]
     everyone += [at_z(d) for d in range(1, NZ)] + [sibling]
     for device in everyone:
         pl.semaphore_signal(barrier, inc=1, device_id=device, device_id_type=MESH)
+    load = pltpu.make_async_copy(momentum_hbm, momentum, load_sem)
+    load.start()
+    weights_load = pltpu.make_async_copy(weights_hbm, weights, weights_sem)
+    weights_load.start()
 
     stage[...] = jnp.zeros_like(stage)
     basis_load.wait()
@@ -138,8 +140,6 @@
         width = min(512, COLS - 512 * q)
         stage[4 * q : 4 * q + 4, :width] = basis[:, 512 * q : 512 * q + width]
     slots[f] = stage[...].astype(BF16)
-    load.wait()
-    weights_load.wait()
     pl.semaphore_wait(barrier, len(everyone))
 
     for d in FAR_FIRST:
@@ -152,26 +152,27 @@
         for d in (2, 1, 3):
             send(slots.at[source], slots.at[source], slot_send, slot_x_recv.at[d], at_x(d))
     later(slots.at[pl.ds(0, 31)], slot_send)
-    for d in range(1, NX):
-        wait(slots.at[pl.ds(((x - d) % NX) * NY, NY)], slot_x_recv.at[d])
-
-    flat = slots[...].reshape(512, 512)
-    to_row = lax.broadcasted_iota(jnp.int32, (RANK, 512), 0)
-    from_row = lax.broadcasted_iota(jnp.int32, (RANK, 512), 1)
-    parts = []
-    for q in range(4):
-        width = min(512, COLS - 512 * q)
-        pick = (from_row == (to_row // 4) * 16 + 4 * q + to_row % 4).astype(F32).astype(BF16)
-        parts.append(jnp.dot(pick, flat[:, :width], preferred_element_type=F32).astype(BF16))
-
-    def product(half):
-        total = None
+    to_row = lax.broadcasted_iota(jnp.int32, (NY * 4, RANK), 0)
+    from_row = lax.broadcasted_iota(jnp.int32, (NY * 4, RANK), 1)
+
+    def arrange(d):
+        group = (x - d) % NX
+        flat = slots[pl.ds(group * NY, NY)].reshape(RANK, 512)
         for q in range(4):
             width = min(512, COLS - 512 * q)
-            block = momentum[pl.ds(half * (ROWS // 2), ROWS // 2), 512 * q : 512 * q + width]
-            term = lax.dot_general(block, parts[q], (((1,), (1,)), ((), ())), preferred_element_type=F32)
-            total = term if total is None else total + term
-        return total
+            pick = (from_row == (to_row // 4) * 16 + 4 * q + to_row % 4).astype(F32).astype(BF16)
+            part = jnp.dot(pick, flat[:, :width], preferred_element_type=F32).astype(BF16)
+            full_basis[pl.ds(pl.multiple_of(group * NY * 4, 32), NY * 4), 512 * q : 512 * q + width] = part
+
+    arrange(0)
+    load.wait()
+    for d in (1, 3, 2):
+        wait(slots.at[pl.ds(((x - d) % NX) * NY, NY)], slot_x_recv.at[d])
+        arrange(d)
+
+    def product(half):
+        block = momentum[pl.ds(half * (ROWS // 2), ROWS // 2), :]
+        return lax.dot_general(block, full_basis[...], ACROSS, preferred_element_type=F32)
 
     partial[other] = product(other)
     for e in FAR_FIRST + (0,):
@@ -188,6 +189,7 @@
     rows = pl.ds(z * 16, 16)
     wait(pair_in.at[rows], pair_recv.at[0])
     total = partial[c, rows, :] + pair_in[rows, :]
+    momentum_t[...] = momentum[...].T
     wait(sum_in, sum_recv)
     for d in range(NZ - 1):
         total = total + sum_in[d]
@@ -216,9 +218,8 @@
     low = (left - mid.astype(F32)).astype(BF16)
     terms = jnp.concatenate([hi, mid, low], axis=1)
     for piece in range(NX):
-        out = lax.dot_general(
-            momentum[:, QUARTER * piece : QUARTER * (piece + 1)], terms, (((0,), (0,)), ((), ())),
-            preferred_element_type=F32,
+        out = jnp.dot(
+            momentum_t[QUARTER * piece : QUARTER * (piece + 1), :], terms, preferred_element_type=F32
         )
         out = out[:, :RANK] + out[:, RANK : 2 * RANK] + out[:, 2 * RANK :]
         for n in range(NSLOT):
@@ -227,22 +228,31 @@
 
     def send_slot(e):
         slot = (y + e) % NY
+        step = 1 + 2 * (slot % 2)
 
         @pl.when(slot < NSLOT)
         def _():
-            for d in (2, 1, 3):
-                send(zq.at[(x + d) % NX, slot], zx.at[x, slot], zx_send, zx_recv.at[e], at_x(d))
+            send(zq.at[(x + 2) % NX, slot], zfar.at[e], zx_send.at[0], zfar_recv.at[e], at_x(step))
+            send(zq.at[(x + NX - step) % NX, slot], zx.at[0, slot], zx_send.at[1], zx_recv.at[e], at_x(NX - step))
+
+    def pass_slot(e):
+        slot = (y + e) % NY
+        step = 1 + 2 * (slot % 2)
+        target = (x + step) % NX
+
+        @pl.when(slot < NSLOT)
+        def _():
+            wait(zfar.at[e], zfar_recv.at[e])
+            zq[target, slot] = zq[target, slot] + zfar[e]
+            send(zq.at[target, slot], zx.at[1, slot], zx_send.at[2], zx_recv.at[e], at_x(step))
 
     def reduce_slot(e):
         slot = (y + e) % NY
 
         @pl.when(slot < NSLOT)
         def _():
-            wait(zx.at[pl.ds(0, 3), 0], zx_recv.at[e])
-            total = zq[x, slot]
-            for d in range(1, NX):
-                total = total + zx[(x + d) % NX, slot]
-            zmid[slot] = total
+            wait(zx.at[pl.ds(0, 2), 0], zx_recv.at[e])
+            zmid[slot] = zq[x, slot] + zx[0, slot] + zx[1, slot]
             if e:
                 send(zmid.at[slot], zy.at[e - 1], zy_send.at[e], zy_recv, at_y(e))
 
@@ -252,7 +262,9 @@
     slot_order = FAR_FIRST + (0,)
     for e in slot_order:
         send_slot(e)
-    later(zx.at[pl.ds(0, 3)], zx_send)
+    later(zfar.at[pl.ds(0, NSLOT)], zx_send.at[0])
+    later(zx.at[0], zx_send.at[1])
+    later(zx.at[1], zx_send.at[2])
 
     wait(gram_x, gx_recv)
     own = 2 * x + c
@@ -260,6 +272,8 @@
     for d in FAR_FIRST:
         send(gram_mid, gram_y.at[d - 1], gy_send, gy_recv, at_y(d))
     later(gram_y, gy_send)
+    for e in slot_order:
+        pass_slot(e)
     for e in slot_order[:2]:
         reduce_slot(e)
     wait(gram_y, gy_recv)
@@ -274,12 +288,11 @@
             device = (((x + d) % NX) * NY + y, z * 2 + core)
             send(gram_full.at[own], gram_full.at[own], ga_send, ga_recv, device)
     later(gram_full.at[pl.ds(0, 7)], ga_send)
-    for e in slot_order[2:5]:
+    for e in slot_order[2:7]:
         reduce_slot(e)
     wait(gram_full.at[pl.ds(0, 7)], ga_recv)
 
-    between = {5: functools.partial(reduce_slot, slot_order[5]), 8: functools.partial(reduce_slot, slot_order[6])}
-    inverse = inverse_factor(gram_full[...].reshape(RANK, RANK), between)
+    inverse = inverse_factor(gram_full[...].reshape(RANK, RANK))
     reduce_slot(0)
     holder = y < NSLOT
 
@@ -341,6 +354,7 @@
         gathered(d)
     feedback = lax.dot_general(ortho.astype(BF16), whole[...], ACROSS, preferred_element_type=F32)
     momentum_out[...] = (momentum[...].astype(F32) - 0.05 * feedback).astype(BF16)
+    weights_load.wait()
     wait(sq_f_in, sq_recv.at[1])
     squares = sq_f[...] + jnp.sum(sq_f_in[...], axis=0)
     scale = lax.rsqrt(squares / FW + 1e-06)
@@ -380,10 +394,12 @@
         out_specs=(vmem, vmem, vmem),
         scratch_shapes=[
             pltpu.VMEM((ROWS, COLS), BF16),
+            pltpu.VMEM((COLS, ROWS), BF16),
             pltpu.VMEM((ROWS, COLS), F32),
             pltpu.VMEM((4, COLS), F32),
             pltpu.VMEM((16, 512), F32),
             pltpu.VMEM((32, 16, 512), BF16),
+            pltpu.VMEM((RANK, COLS), BF16),
             pltpu.VMEM((2, ROWS // 2, RANK), F32),
             pltpu.VMEM((ROWS // 2, RANK), F32),
             pltpu.VMEM((NZ - 1, 16, RANK), F32),
@@ -394,7 +410,8 @@
             pltpu.VMEM((NY - 1, 16, RANK), F32),
             pltpu.VMEM((8, 16, RANK), F32),
             pltpu.VMEM((NX, NSLOT, SLOT, RANK), F32),
-            pltpu.VMEM((NX, NSLOT, SLOT, RANK), F32),
+            pltpu.VMEM((NY, SLOT, RANK), F32),
+            pltpu.VMEM((2, NSLOT, SLOT, RANK), F32),
             pltpu.VMEM((NSLOT, SLOT, RANK), F32),
             pltpu.VMEM((NY - 1, SLOT, RANK), F32),
             pltpu.VMEM((NX, NSLOT, SLOT, RANK), BF16),
@@ -405,7 +422,7 @@
             pltpu.VMEM((NX * NY - 1, 1, RANK), F32),
             dma(()), dma(()), dma(()), dma((NY,)), dma((NX,)), dma(()), dma((NZ,)), dma(()), dma(()), dma(()),
             dma((NZ,)), dma(()), dma(()), dma(()), dma(()), dma(()), dma(()), dma(()), dma(()), dma(()),
-            dma((NY,)), dma(()), dma(()), dma((NY,)), dma((NY,)), dma((NX,)), dma((2,)), dma((2,)), dma((2,)),
+            dma((NY,)), dma((NY,)), dma((3,)), dma(()), dma((NY,)), dma((NY,)), dma((NX,)), dma((2,)), dma((2,)), dma((2,)),
         ],
         compiler_params=pltpu.CompilerParams(
             collective_id=0, has_side_effects=True, vmem_limit_bytes=48 * 2**20

time: 71 us -> 68.6 us (0.966)
  Pallas kernels: 70.2 us -> 67.8 us
    pallas_call x1, Pallas kernels: 68.7 us -> 66.3 us  [shards(): pl.pallas_call(exchange_kernel, out_shape=(jax.ShapeDtypeStruct((ROWS, CO...]
where the time goes in v3:
time: 68.6 us; the launch traced here: 68.4 us
  Pallas kernels  67.8 us (99%)
    pallas_call x1, Pallas kernels, shards(): pl.pallas_call(exchange_kernel, out_shape=(jax.ShapeDtypeStruct((ROWS, CO...  66.3 us
    pallas_call x1, Pallas kernels, shards(): pl.pallas_call(place_kernel, out_shape=(jax.ShapeDtypeStruct((ROWS, COLS)...  1.49 us

profile of v3, /device:TPU:1, one launch (start us, length us, event | category | flops | bytes accessed | tf_op | source)
XLA Modules:
  0.0 68.4 jit_solution(69406210983491251)
XLA Ops:
  0.6 66.3 %exchange.1 = (f32[256,1664]{1,0:T(8,128)S(1)}, bf16[256,1664]{1,0:T(8,128)(2,1)S(1)}, f32[4,1664]{1,0:T(4,128)S(1)}) custom-call(bf16[256,1664]{1,0:T(8,128)(2,1)} %momentum_hbm.1, f32[256,1664]{1,0:T(8,128)} %weights_hbm.1, f32[4,1664]{1,0:T(4,128)} %bitcast.2), custom_call_target="tpu_custom_call" | custom-call | tf_op jit(solution)/shard_map/exchange/pallas_call | solution.py:386
  67.0 1.5 %place.1 = (f32[256,1664]{1,0:T(8,128)}, bf16[256,1664]{1,0:T(8,128)(2,1)}, f32[4,1664]{1,0:T(4,128)}) custom-call(f32[256,1664]{1,0:T(8,128)S(1)} %get-tuple-element.9.weights, bf16[256,1664]{1,0:T(8,128)(2,1)S(1)} %get-tuple-element.10.momentum, f32[4,1664]{1,0:T(4,128)S(1)} %get-tuple-element.11.basis), custom_call_target="tpu_custom_call" | custom-call | tf_op jit(solution)/shard_map/place/pallas_call | solution.py:432

commit v4 on v3

--- a/solution.py
+++ b/solution.py
@@ -125,8 +125,7 @@
     basis_load = pltpu.make_async_copy(basis_hbm, basis, basis_sem)
     basis_load.start()
     barrier = pltpu.get_barrier_semaphore()
-    everyone = [at_y(d) for d in range(1, NY)] + [at_x(d) for d in range(1, NX)]
-    everyone += [at_z(d) for d in range(1, NZ)] + [sibling]
+    everyone = [at(d) for d in FAR_FIRST for at in (at_y, at_z)] + [at_x(d) for d in (2, 1, 3)] + [sibling]
     for device in everyone:
         pl.semaphore_signal(barrier, inc=1, device_id=device, device_id_type=MESH)
     load = pltpu.make_async_copy(momentum_hbm, momentum, load_sem)
@@ -142,10 +141,10 @@
     slots[f] = stage[...].astype(BF16)
     pl.semaphore_wait(barrier, len(everyone))
 
-    for d in FAR_FIRST:
-        send(slots.at[f], slots.at[f], slot_send, slot_y_recv.at[d], at_y(d))
     for d in (2, 1, 3):
         send(slots.at[f], slots.at[f], slot_send, slot_x_recv.at[d], at_x(d))
+    for d in NEAR_FIRST:
+        send(slots.at[f], slots.at[f], slot_send, slot_y_recv.at[d], at_y(d))
     for e in NEAR_FIRST:
         source = x * NY + (y - e) % NY
         wait(slots.at[source], slot_y_recv.at[e])
@@ -305,10 +304,10 @@
         mine = lax.dot_general(total, inverse, (((1,), (1,)), ((), ())), precision=HIGH, preferred_element_type=F32)
         mine = mine.astype(BF16)
         back[x, y] = mine
-        for d in FAR_FIRST:
-            send(back.at[x, y], back.at[x, y], t_send.at[0], ty_recv.at[d], at_y(d))
         for d in (2, 1, 3):
             send(back.at[x, y], back.at[x, y], t_send.at[0], tx_recv.at[d], at_x(d))
+        for d in NEAR_FIRST:
+            send(back.at[x, y], back.at[x, y], t_send.at[0], ty_recv.at[d], at_y(d))
         mine = mine.astype(F32)
         sq_t[...] = jnp.sum(mine * mine, axis=0, keepdims=True)
 

time: 68.6 us -> 67.6 us (0.985)
  Pallas kernels: 67.8 us -> 66.8 us
    pallas_call x1, Pallas kernels: 66.3 us -> 65.3 us  [shards(): pl.pallas_call(exchange_kernel, out_shape=(jax.ShapeDtypeStruct((ROWS, CO...]
where the time goes in v4:
time: 67.6 us; the launch traced here: 67.4 us
  Pallas kernels  66.8 us (99%)
    pallas_call x1, Pallas kernels, shards(): pl.pallas_call(exchange_kernel, out_shape=(jax.ShapeDtypeStruct((ROWS, CO...  65.3 us
    pallas_call x1, Pallas kernels, shards(): pl.pallas_call(place_kernel, out_shape=(jax.ShapeDtypeStruct((ROWS, COLS)...  1.49 us

profile of v4, /device:TPU:1, one launch (start us, length us, event | category | flops | bytes accessed | tf_op | source)
XLA Modules:
  0.0 67.4 jit_solution(17443461535971246387)
XLA Ops:
  0.6 65.3 %exchange.1 = (f32[256,1664]{1,0:T(8,128)S(1)}, bf16[256,1664]{1,0:T(8,128)(2,1)S(1)}, f32[4,1664]{1,0:T(4,128)S(1)}) custom-call(bf16[256,1664]{1,0:T(8,128)(2,1)} %momentum_hbm.1, f32[256,1664]{1,0:T(8,128)} %weights_hbm.1, f32[4,1664]{1,0:T(4,128)} %bitcast.2), custom_call_target="tpu_custom_call" | custom-call | tf_op jit(solution)/shard_map/exchange/pallas_call | solution.py:385
  66.0 1.5 %place.1 = (f32[256,1664]{1,0:T(8,128)}, bf16[256,1664]{1,0:T(8,128)(2,1)}, f32[4,1664]{1,0:T(4,128)}) custom-call(f32[256,1664]{1,0:T(8,128)S(1)} %get-tuple-element.9.weights, bf16[256,1664]{1,0:T(8,128)(2,1)S(1)} %get-tuple-element.10.momentum, f32[4,1664]{1,0:T(4,128)S(1)} %get-tuple-element.11.basis), custom_call_target="tpu_custom_call" | custom-call | tf_op jit(solution)/shard_map/place/pallas_call | solution.py:431

commit v5 on v4

--- a/solution.py
+++ b/solution.py
@@ -201,12 +201,17 @@
         source = (z - d) % NZ
         wait(projected.at[c, source], own_recv.at[d])
         send(projected.at[c, source], projected.at[c, source], half_send, half_recv, sibling)
+
+    def gram_of(half):
+        rows = projected[half].reshape(ROWS // 2, RANK)
+        return lax.dot_general(rows, rows, (((0,), (0,)), ((), ())), precision=HIGH, preferred_element_type=F32)
+
+    gram = gram_of(c)
     wait(projected.at[other], half_recv)
     later(projected.at[c], half_send)
 
     proj = projected[...].reshape(ROWS, RANK)
-    gram = lax.dot_general(proj, proj, (((0,), (0,)), ((), ())), precision=HIGH, preferred_element_type=F32)
-    gram_buf[...] = gram.reshape(8, 16, RANK)
+    gram_buf[...] = (gram + gram_of(other)).reshape(8, 16, RANK)
     for d in range(1, NX):
         send(gram_buf.at[2 * ((x + d) % NX) + c], gram_x.at[d - 1], gx_send, gx_recv, at_x(d))
     later(gram_x, gx_send)
@@ -329,7 +334,7 @@
             for d in (2, 1, 3):
                 send(back.at[x, source], back.at[x, source], t_send.at[1], tx_recv.at[d], at_x(d))
 
-    for e in NEAR_FIRST[:6]:
+    for e in NEAR_FIRST[:5]:
         relay(e)
     wait(sq_t_in, sq_recv.at[0])
     sq_f[...] = sq_t[...] + jnp.sum(sq_t_in[...], axis=0)
@@ -339,7 +344,8 @@
                 device = (((x + dx) % NX) * NY + (y + dy) % NY, t)
                 send(sq_f, sq_f_in.at[dx * NY + dy - 1], sq_send.at[1], sq_recv.at[1], device)
     later(sq_f_in, sq_send.at[1])
-    relay(NEAR_FIRST[6])
+    for e in NEAR_FIRST[5:]:
+        relay(e)
     later(slots.at[pl.ds(0, 10)], t_send.at[0], holder)
     later(slots.at[pl.ds(0, 18)], t_send.at[1], holder)
     later(slots.at[pl.ds(0, 21)], t_send.at[1], jnp.logical_not(holder))

time: 67.6 us -> 67.8 us (level)
  no operation moved by 1% of the time
where the time goes in v5:
time: 67.8 us; the launch traced here: 67.7 us
  Pallas kernels  67 us (99%)
    pallas_call x1, Pallas kernels, shards(): pl.pallas_call(exchange_kernel, out_shape=(jax.ShapeDtypeStruct((ROWS, CO...  65.5 us
    pallas_call x1, Pallas kernels, shards(): pl.pallas_call(place_kernel, out_shape=(jax.ShapeDtypeStruct((ROWS, COLS)...  1.49 us

profile of v5, /device:TPU:1, one launch (start us, length us, event | category | flops | bytes accessed | tf_op | source)
XLA Modules:
  0.0 67.7 jit_solution(15702350669185881156)
XLA Ops:
  0.6 65.5 %exchange.1 = (f32[256,1664]{1,0:T(8,128)S(1)}, bf16[256,1664]{1,0:T(8,128)(2,1)S(1)}, f32[4,1664]{1,0:T(4,128)S(1)}) custom-call(bf16[256,1664]{1,0:T(8,128)(2,1)} %momentum_hbm.1, f32[256,1664]{1,0:T(8,128)} %weights_hbm.1, f32[4,1664]{1,0:T(4,128)} %bitcast.2), custom_call_target="tpu_custom_call" | custom-call | tf_op jit(solution)/shard_map/exchange/pallas_call | solution.py:391
  66.2 1.5 %place.1 = (f32[256,1664]{1,0:T(8,128)}, bf16[256,1664]{1,0:T(8,128)(2,1)}, f32[4,1664]{1,0:T(4,128)}) custom-call(f32[256,1664]{1,0:T(8,128)S(1)} %get-tuple-element.9.weights, bf16[256,1664]{1,0:T(8,128)(2,1)S(1)} %get-tuple-element.10.momentum, f32[4,1664]{1,0:T(4,128)S(1)} %get-tuple-element.11.basis), custom_call_target="tpu_custom_call" | custom-call | tf_op jit(solution)/shard_map/place/pallas_call | solution.py:437

commit v6 on v4

--- a/solution.py
+++ b/solution.py
@@ -18,6 +18,7 @@
 SLOT = 64
 AHEAD = 3
 NSLOT = 7
+LAST = QUARTER - (NSLOT - 1) * SLOT
 FAR_FIRST = (4, 3, 5, 2, 6, 1, 7)
 NEAR_FIRST = (1, 7, 2, 6, 3, 5, 4)
 
@@ -304,10 +305,15 @@
         mine = lax.dot_general(total, inverse, (((1,), (1,)), ((), ())), precision=HIGH, preferred_element_type=F32)
         mine = mine.astype(BF16)
         back[x, y] = mine
-        for d in (2, 1, 3):
-            send(back.at[x, y], back.at[x, y], t_send.at[0], tx_recv.at[d], at_x(d))
-        for d in NEAR_FIRST:
-            send(back.at[x, y], back.at[x, y], t_send.at[0], ty_recv.at[d], at_y(d))
+
+        def spread(slot):
+            for d in (2, 1, 3):
+                send(slot, slot, t_send.at[0], tx_recv.at[d], at_x(d))
+            for d in NEAR_FIRST:
+                send(slot, slot, t_send.at[0], ty_recv.at[d], at_y(d))
+
+        pl.when(y < NSLOT - 1)(lambda: spread(back.at[x, y]))
+        pl.when(y == NSLOT - 1)(lambda: spread(back.at[x, NSLOT - 1, pl.ds(0, LAST)]))
         mine = mine.astype(F32)
         sq_t[...] = jnp.sum(mine * mine, axis=0, keepdims=True)
 
@@ -323,11 +329,13 @@
     def relay(e):
         source = (y - e) % NY
 
-        @pl.when(source < NSLOT)
-        def _():
-            wait(back.at[x, source], ty_recv.at[e])
+        def step(slot):
+            wait(slot, ty_recv.at[e])
             for d in (2, 1, 3):
-                send(back.at[x, source], back.at[x, source], t_send.at[1], tx_recv.at[d], at_x(d))
+                send(slot, slot, t_send.at[1], tx_recv.at[d], at_x(d))
+
+        pl.when(source < NSLOT - 1)(lambda: step(back.at[x, source]))
+        pl.when(source == NSLOT - 1)(lambda: step(back.at[x, NSLOT - 1, pl.ds(0, LAST)]))
 
     for e in NEAR_FIRST[:6]:
         relay(e)
@@ -340,13 +348,15 @@
                 send(sq_f, sq_f_in.at[dx * NY + dy - 1], sq_send.at[1], sq_recv.at[1], device)
     later(sq_f_in, sq_send.at[1])
     relay(NEAR_FIRST[6])
-    later(slots.at[pl.ds(0, 10)], t_send.at[0], holder)
-    later(slots.at[pl.ds(0, 18)], t_send.at[1], holder)
-    later(slots.at[pl.ds(0, 21)], t_send.at[1], jnp.logical_not(holder))
+    later(whole.at[pl.ds(0, 10 * SLOT)], t_send.at[0], y < NSLOT - 1)
+    later(whole.at[pl.ds(0, 10 * LAST)], t_send.at[0], y == NSLOT - 1)
+    later(whole.at[pl.ds(0, 3 * (QUARTER - SLOT))], t_send.at[1], y < NSLOT - 1)
+    later(whole.at[pl.ds(0, 3 * (QUARTER - LAST))], t_send.at[1], y == NSLOT - 1)
+    later(whole.at[pl.ds(0, 3 * QUARTER)], t_send.at[1], jnp.logical_not(holder))
     def gathered(d):
         piece = (x - d) % NX
         if d:
-            wait(back.at[piece], tx_recv.at[d])
+            wait(whole.at[pl.ds(0, QUARTER)], tx_recv.at[d])
         whole[pl.ds(pl.multiple_of(piece * QUARTER, 32), QUARTER), :] = back[piece].reshape(NSLOT * SLOT, RANK)[:QUARTER, :]
 
     for d in (0, 1, 3, 2):

time: 67.6 us -> 67.4 us (level)
  no operation moved by 1% of the time
where the time goes in v6:
time: 67.4 us; the launch traced here: 67.3 us
  Pallas kernels  66.6 us (99%)
    pallas_call x1, Pallas kernels, shards(): pl.pallas_call(exchange_kernel, out_shape=(jax.ShapeDtypeStruct((ROWS, CO...  65.1 us
    pallas_call x1, Pallas kernels, shards(): pl.pallas_call(place_kernel, out_shape=(jax.ShapeDtypeStruct((ROWS, COLS)...  1.49 us

profile of v6, /device:TPU:1, one launch (start us, length us, event | category | flops | bytes accessed | tf_op | source)
XLA Modules:
  0.0 67.3 jit_solution(12199163392886171900)
XLA Ops:
  0.6 65.1 %exchange.1 = (f32[256,1664]{1,0:T(8,128)S(1)}, bf16[256,1664]{1,0:T(8,128)(2,1)S(1)}, f32[4,1664]{1,0:T(4,128)S(1)}) custom-call(bf16[256,1664]{1,0:T(8,128)(2,1)} %momentum_hbm.1, f32[256,1664]{1,0:T(8,128)} %weights_hbm.1, f32[4,1664]{1,0:T(4,128)} %bitcast.2), custom_call_target="tpu_custom_call" | custom-call | tf_op jit(solution)/shard_map/exchange/pallas_call | solution.py:395
  65.8 1.5 %place.1 = (f32[256,1664]{1,0:T(8,128)}, bf16[256,1664]{1,0:T(8,128)(2,1)}, f32[4,1664]{1,0:T(4,128)}) custom-call(f32[256,1664]{1,0:T(8,128)S(1)} %get-tuple-element.9.weights, bf16[256,1664]{1,0:T(8,128)(2,1)S(1)} %get-tuple-element.10.momentum, f32[4,1664]{1,0:T(4,128)S(1)} %get-tuple-element.11.basis), custom_call_target="tpu_custom_call" | custom-call | tf_op jit(solution)/shard_map/place/pallas_call | solution.py:441
